TPU v7x, 32 devices: a whole 2x2x4 slice. The times are simulated.
32 devices in a mesh: sector: 4 (over z), op: 8 (over y, x, core).
Axes of the slice: x: 2, y: 2, z: 4, core: 2. Of those that a mesh axis runs over, the one named last changes fastest.
Arguments:
- wavefunction: float32 [4, 512, 512], P('sector', 'op'), may hold values from -6 to 6
- diagonal: float32 [4, 512, 512], P('sector', 'op'), may hold values from 2 to 10
- left_blocks: bfloat16 [64, 512, 512], P('op'), may hold values from -1 to 1
- right_blocks: bfloat16 [64, 512, 512], P('op'), may hold values from -1 to 1
- coupling: int32 [4, 64], replicated, may hold values from 0 to 3
- sector_sizes: int32 [4], replicated, may hold values from 256 to 512
Outputs:
- vector: float32 [4, 512, 512], P('sector', 'op')
- energies: float32 [2], replicated
All inputs are finite; a program needn't handle non-finite values.
Results may differ from a plain program's by a relative error of at most 0.0052.
Values may be sent and summed in bfloat16 or wider, within the bound.
A program may use at most 64 MiB of HBM per device.

v0:
```python
import jax
import jax.numpy as jnp
from jax import lax
from jax.sharding import PartitionSpec as P

STEPS = 2


def shards(wavefunction, diagonal, left_blocks, right_blocks, coupling, sector_sizes):
    sector_count, share_rows, block_width = wavefunction.shape
    pair_count = left_blocks.shape[0]
    op_count = lax.axis_size("op")
    sector_place = lax.axis_index("sector")
    op_place = lax.axis_index("op")
    first_sector = sector_place * sector_count
    my_coupling = lax.dynamic_slice_in_dim(coupling, first_sector, sector_count, 0)
    my_sizes = lax.dynamic_slice_in_dim(sector_sizes, first_sector, sector_count, 0)
    columns = jnp.arange(block_width, dtype=jnp.int32)
    row_ids = op_place * share_rows + jnp.arange(share_rows, dtype=jnp.int32)
    bound = my_sizes[:, None, None]
    share_mask = ((row_ids[None, :, None] < bound) & (columns[None, None, :] < bound)).astype(
        jnp.float32
    )
    full_mask = ((columns[None, :, None] < bound) & (columns[None, None, :] < bound)).astype(
        jnp.float32
    )
    entry_total = float(wavefunction.size * lax.axis_size("sector") * op_count)
    current = wavefunction * share_mask
    collected = []
    for iteration in range(STEPS):
        current_low = current.astype(jnp.bfloat16)
        rows_all = lax.all_gather(current_low, "sector", axis=0, tiled=True)
        whole = lax.all_gather(rows_all, "op", axis=1, tiled=True)
        wanted = lax.dynamic_slice_in_dim(my_coupling, op_place * pair_count, pair_count, 1)
        sources = jnp.take(whole, wanted.reshape(-1), axis=0)
        sources = sources.reshape(sector_count, pair_count, block_width, block_width)
        half = jnp.einsum(
            "bij,abjk->abik", left_blocks, sources, preferred_element_type=jnp.float32
        ).astype(jnp.bfloat16)
        partial_terms = (
            jnp.einsum("abik,blk->ail", half, right_blocks, preferred_element_type=jnp.float32)
            * full_mask
        )
        sigma_share = lax.psum_scatter(partial_terms, "op", scatter_dimension=1, tiled=True)
        numerator, denominator = lax.psum(
            (jnp.sum(current * sigma_share), jnp.sum(current * current)), ("sector", "op")
        )
        theta = numerator / (denominator + 1e-06)
        collected.append(theta)
        gap = diagonal - theta
        update = current - (sigma_share - theta * current) * gap / (gap * gap + 1.0)
        squares = lax.psum(jnp.sum(update * update), ("sector", "op"))
        current = update * lax.rsqrt(squares / entry_total + 1e-06)
    return (current, jnp.stack(collected))


def solution(mesh):
    in_specs = (
        P("sector", "op", None),
        P("sector", "op", None),
        P("op", None, None),
        P("op", None, None),
        P(),
        P(),
    )
    out_specs = (P("sector", "op", None), P())
    return jax.shard_map(shards, mesh=mesh, in_specs=in_specs, out_specs=out_specs, check_vma=False)
```

profile of v0, /device:TPU:0, one launch (start us, length us, event | category | flops | bytes accessed | tf_op | source)
XLA Modules:
  0.0 382.1 jit_solution(6063786722842393509)
XLA Ops:
  7.2 0.0 all-gather.3.cloned.1.call-start
  7.2 1.2 dynamic_slice.8
  8.5 0.6 iota_compare_fusion
  9.1 0.7 add_compare_fusion
  9.8 1.0 fusion.38
  10.8 16.3 %all_gather.12 = bf16[4,64,512]{2,1,0:T(8,128)(2,1)} all-gather(bf16[1,64,512]{2,1,0:T(8,128)(2,1)S(1)} %fusion.38), channel_id=1, replica_groups=mesh['sector'=4,'op'=8] {'sector'}, dimensions={0}, use_global_device_ids=true | all-gather | bytes 327680 | tf_op jit(solution)/shard_map/all_gather | solution.py:32
  27.1 0.0 all-gather.3.cloned.1.call-update
  27.1 0.0 reduce-scatter.3.cloned.1.call-start
  27.2 0.8 compare_and_fusion
  28.0 28.8 %all-gather.3.cloned.1.call-done = bf16[4,512,512]{2,1,0:T(8,128)(2,1)} async-done(((bf16[4,64,512]{2,1,0:T(8,128)(2,1)}), bf16[4,512,512]{2,1,0:T(8,128)(2,1)}) %all-gather.3.cloned.1.call-update) | async-done | bytes 2097168 | tf_op jit(solution)/shard_map/all_gather | solution.py:33
  56.7 4.3 %gather_fusion = bf16[8,512,512]{2,1,0:T(8,128)(2,1)} fusion(bf16[4,512,512]{2,1,0:T(8,128)(2,1)} %all-gather.3.cloned.1.call-done, s32[1024]{0:T(1024)S(1)} %pad_clamp_fusion), kind=kCustom, calls=%fused_computation.clone | custom fusion | bytes 8388640 | tf_op jit(solution)/shard_map/jit(_take)/gather | solution.py:35
  61.1 10.4 %fusion.27 = f32[1,512,512]{2,1,0:T(8,128)} fusion(bf16[8,512,512]{2,1,0:T(8,128)(2,1)} %param.11, pred[512]{0:T(512)(128)(4,1)S(1)} %iota_compare_fusion, bf16[8,512,512]{2,1,0:T(8,128)(2,1)} %param.10, bf16[8,512,512]{2,1,0:T(8,128)(2,1)} %gather_fusion, pred[8]{0:T(512)(128)(4,1)S(1)} %get-tuple-element.15), kind=kOutput, calls=%fused_computation.21 | convolution fusion | flops 4299685888 | bytes 13632008 | tf_op jit(solution)/shard_map/abik,blk->ail/dot_general | solution.py:41
  71.5 0.0 reduce-scatter.3.cloned.1.call-update
  71.5 0.0 all-gather.5.cloned.1.call-start
  71.6 36.1 %reduce-scatter.3.cloned.1.call-done = f32[1,64,512]{2,1,0:T(8,128)} async-done(((f32[1,512,512]{2,1,0:T(8,128)}), f32[1,64,512]{2,1,0:T(8,128)}) %reduce-scatter.3.cloned.1.call-update) | async-done | bytes 131088 | tf_op jit(solution)/shard_map/reduce_scatter | solution.py:44
  107.7 1.6 multiply_reduce_fusion.4
  109.3 39.6 %all-reduce.1 = (f32[]{:T(128)}, f32[]{:T(128)}) all-reduce(f32[]{:T(128)} %get-tuple-element.4, f32[]{:T(128)} %get-tuple-element.3), channel_id=1, replica_groups=mesh['sector'=4,'op'=8] {'sector','op'}, use_global_device_ids=true, to_apply=%region_2.4 | all-reduce | flops 2 | bytes 16 | tf_op jit(solution)/shard_map/psum | solution.py:45
  150.2 1.6 multiply_reduce_fusion.3
  151.9 41.4 %psum.44 = f32[]{:T(128)} all-reduce(f32[]{:T(128)} %get-tuple-element.13), channel_id=1, replica_groups=mesh['sector'=4,'op'=8] {'sector','op'}, use_global_device_ids=true, to_apply=%region_6.8 | all-reduce | flops 1 | bytes 8 | tf_op jit(solution)/shard_map/psum | solution.py:52
  194.0 14.6 %all_gather.14 = bf16[4,64,512]{2,1,0:T(8,128)(2,1)} all-gather(bf16[1,64,512]{2,1,0:T(8,128)(2,1)S(1)} %multiply_convert_fusion), channel_id=1, replica_groups=mesh['sector'=4,'op'=8] {'sector'}, dimensions={0}, use_global_device_ids=true | all-gather | bytes 327680 | tf_op jit(solution)/shard_map/all_gather | solution.py:32
  208.6 0.0 all-gather.5.cloned.1.call-update
  208.6 0.2 reduce-scatter.5.cloned.1.call-start
  208.8 28.5 %all-gather.5.cloned.1.call-done = bf16[4,512,512]{2,1,0:T(8,128)(2,1)} async-done(((bf16[4,64,512]{2,1,0:T(8,128)(2,1)}), bf16[4,512,512]{2,1,0:T(8,128)(2,1)}) %all-gather.5.cloned.1.call-update) | async-done | bytes 2097168 | tf_op jit(solution)/shard_map/all_gather | solution.py:33
  237.3 4.3 %gather_fusion.1 = bf16[8,512,512]{2,1,0:T(8,128)(2,1)} fusion(bf16[4,512,512]{2,1,0:T(8,128)(2,1)} %all-gather.5.cloned.1.call-done, s32[1024]{0:T(1024)S(1)} %pad_clamp_fusion), kind=kCustom, calls=%fused_computation.1.clone | custom fusion | bytes 8388640 | tf_op jit(solution)/shard_map/jit(_take)/gather | solution.py:35
  241.6 10.4 %fusion.22 = f32[1,512,512]{2,1,0:T(8,128)} fusion(bf16[8,512,512]{2,1,0:T(8,128)(2,1)} %param.11, pred[512]{0:T(512)(128)(4,1)S(1)} %iota_compare_fusion, bf16[8,512,512]{2,1,0:T(8,128)(2,1)} %param.10, bf16[8,512,512]{2,1,0:T(8,128)(2,1)} %gather_fusion.1, pred[8]{0:T(512)(128)(4,1)S(1)} %get-tuple-element.15), kind=kOutput, calls=%fused_computation.20 | convolution fusion | flops 4299685888 | bytes 13632008 | tf_op jit(solution)/shard_map/abik,blk->ail/dot_general | solution.py:41
  252.0 36.2 %reduce-scatter.5.cloned.1.call-done = f32[1,64,512]{2,1,0:T(8,128)} async-done(((f32[1,512,512]{2,1,0:T(8,128)}), f32[1,64,512]{2,1,0:T(8,128)}) %reduce-scatter.5.cloned.1.call-update) | async-done | bytes 131088 | tf_op jit(solution)/shard_map/reduce_scatter | solution.py:44
  288.2 1.5 multiply_reduce_fusion.1
  289.8 39.6 %all-reduce = (f32[]{:T(128)}, f32[]{:T(128)}) all-reduce(f32[]{:T(128)} %get-tuple-element.6, f32[]{:T(128)} %get-tuple-element.5), channel_id=1, replica_groups=mesh['sector'=4,'op'=8] {'sector','op'}, use_global_device_ids=true, to_apply=%region_9.11 | all-reduce | flops 2 | bytes 16 | tf_op jit(solution)/shard_map/psum | solution.py:45
  330.7 1.6 multiply_reduce_fusion
  332.2 41.4 %psum.47 = f32[]{:T(128)} all-reduce(f32[]{:T(128)} %get-tuple-element.11), channel_id=1, replica_groups=mesh['sector'=4,'op'=8] {'sector','op'}, use_global_device_ids=true, to_apply=%region_13.15 | all-reduce | flops 1 | bytes 8 | tf_op jit(solution)/shard_map/psum | solution.py:52
  374.3 0.7 broadcast_multiply_fusion
  374.9 0.6 pad_maximum_fusion
  (7 shorter events, 0.0 us)
Async XLA Ops:
  7.2 49.6 %all-gather.3.cloned.1.call-start = ((), (), s32[]{:S(2)}) async-start(), calls=%async_computation.2 | async-start | bytes 2359296 | tf_op jit(solution)/shard_map/all_gather | solution.py:33
  27.1 80.6 %reduce-scatter.3.cloned.1.call-start = ((), (), s32[]{:S(2)}) async-start(), calls=%async_computation.3 | async-start | bytes 1179648 | tf_op jit(solution)/shard_map/reduce_scatter | solution.py:44
  61.1 46.7 %copy-start = (f32[1,64,512]{2,1,0:T(8,128)S(1)}, f32[1,64,512]{2,1,0:T(8,128)}, u32[]{:S(2)}) copy-start(f32[1,64,512]{2,1,0:T(8,128)} %param.8) | copy-start | bytes 393220
  61.1 89.2 %copy-start.1 = (f32[1,64,512]{2,1,0:T(8,128)S(1)}, f32[1,64,512]{2,1,0:T(8,128)}, u32[]{:S(2)}) copy-start(f32[1,64,512]{2,1,0:T(8,128)} %param.9) | copy-start | bytes 393220
  71.5 165.7 %all-gather.5.cloned.1.call-start = ((), (), s32[]{:S(2)}) async-start(), calls=%async_computation.4 | async-start | bytes 2359296 | tf_op jit(solution)/shard_map/all_gather | solution.py:33
  208.6 79.6 %reduce-scatter.5.cloned.1.call-start = ((), (), s32[]{:S(2)}) async-start(), calls=%async_computation.5 | async-start | bytes 1179648 | tf_op jit(solution)/shard_map/reduce_scatter | solution.py:44
Sparse Core Ops, SparseCore 0:
  27.2 29.4 all-gather.2
  71.7 36.0 reduce-scatter.2
  208.7 28.5 all-gather.4
  252.2 36.0 reduce-scatter.4
where the time goes:
time: 383 us; the launch traced here: 382 us
  blocking collectives  193 us (50%)
  waiting for transfers between devices  130 us (34%)
  matrix products  20.9 us (5%)
  between operations  17.8 us (5%)
  other arithmetic  10.7 us (3%)
  local copies, waits for them, and re-layouts  9.91 us (3%)
    psum x2, blocking collectives, shards(): squares = lax.psum(jnp.sum(update * update), ('sector', 'op'))  82.7 us
    psum x2, blocking collectives, shards(): lax.psum((jnp.sum(current * sigma_share), jnp.sum(current * current)), ('...  79.1 us
    reduce_scatter x2, waiting for transfers between devices, shards(): lax.psum_scatter(partial_terms, 'op', scatter_dimension=1, tiled=True)  72.3 us
    all_gather x2, waiting for transfers between devices, shards(): whole = lax.all_gather(rows_all, 'op', axis=1, tiled=True)  57.2 us
    all_gather x2, blocking collectives, shards(): rows_all = lax.all_gather(current_low, 'sector', axis=0, tiled=True)  30.9 us
    dot_general x2, matrix products, shards(): jnp.einsum('abik,blk->ail', half, right_blocks, preferred_element_type=jn...  20.9 us
    gather x2, local copies, waits for them, and re-layouts, shards(): sources = jnp.take(whole, wanted.reshape(-1), axis=0)  8.66 us
  transfers between devices with their start and end apart: 4, of which 4 were waited for; matrix products, arithmetic and copies ran while one was open for 0% of the time, Pallas kernels for 0%

commit v1 on v0

v1 whole, which is shorter than its diff:
```python
import functools

import jax
import jax.numpy as jnp
from jax import lax
from jax.experimental import pallas as pl
from jax.experimental.pallas import tpu as pltpu
from jax.sharding import PartitionSpec as P

STEPS = 2
MESH = pl.DeviceIdType.MESH
F32 = jnp.float32
BF16 = jnp.bfloat16


def flip(value, mask):
    bit = 1
    while bit <= mask:
        if mask & bit:
            value = value + bit - 2 * bit * ((value // bit) % 2)
        bit *= 2
    return value


def folded(x):
    rows, width = x.shape
    x = jnp.sum(x.reshape(rows // 8, 8, width), axis=0)
    total = x[:, 0:128]
    for at in range(128, width, 128):
        total = total + x[:, at : at + 128]
    return total


def total_of(tile):
    return jnp.sum(jnp.sum(tile, axis=0, keepdims=True), axis=1, keepdims=True)


def kernel(
    sectors, ops, entry_total,
    coup, sizes, wf, diag, left, right,
    vec, energies,
    lv, rv, xa, xb, tt, acc, cur, s1_tx, s1_rx, s2_tx, s2_rx, sc_a, sc_b, sc_t,
    load_sem, x_send, x_recv, r1_send, r1_recv, r2_send, r2_recv, a_send, a_recv, b_send, b_recv,
):
    rows, width = wf.shape
    pairs = left.shape[0]
    chips = ops // 2
    half = chips // 2
    bits = chips.bit_length() - 1
    half_rows = half * 2 * rows
    z = lax.axis_index("sector")
    o = lax.axis_index("op")
    m, c = o // 2, o % 2
    top = m // half

    loads = [
        pltpu.make_async_copy(right, rv, load_sem.at[0]),
        pltpu.make_async_copy(left, lv, load_sem.at[1]),
    ]
    for load in loads:
        load.start()

    barrier = pltpu.get_barrier_semaphore()
    for k in range(1, ops):
        pl.semaphore_signal(barrier, inc=1, device_id=(z, flip(o, k)), device_id_type=MESH)
    for d in range(1, sectors):
        pl.semaphore_signal(barrier, inc=1, device_id=(flip(z, d), o), device_id_type=MESH)

    bound = sizes[z]
    row_ids = o * rows + lax.broadcasted_iota(jnp.int32, (rows, width), 0)
    col_ids = lax.broadcasted_iota(jnp.int32, (rows, width), 1)
    mask = ((row_ids < bound) & (col_ids < bound)).astype(F32)
    cur[...] = wf[...] * mask
    pl.semaphore_wait(barrier, ops - 1 + sectors - 1)

    def reduce_tile(red):
        sent = []
        for k in range(1, ops):
            copy = pltpu.make_async_remote_copy(
                sc_t.at[red], sc_a.at[red, o], a_send.at[red, k], a_recv.at[red, k],
                device_id=(z, flip(o, k)), device_id_type=MESH)
            copy.start()
            sent.append(copy)
        sc_a[red, o] = sc_t[red]

        def finish():
            for k in range(1, ops):
                pltpu.make_async_remote_copy(
                    sc_t.at[red], sc_a.at[red, flip(o, k)], a_send.at[red, k], a_recv.at[red, k],
                    device_id=(z, flip(o, k)), device_id_type=MESH).wait_recv()
            sc_b[red, z] = jnp.sum(sc_a[red], axis=0)
            for d in range(1, sectors):
                copy = pltpu.make_async_remote_copy(
                    sc_b.at[red, z], sc_b.at[red, z], b_send.at[red, d], b_recv.at[red, d],
                    device_id=(flip(z, d), o), device_id_type=MESH)
                copy.start()
                sent.append(copy)
            for d in range(1, sectors):
                pltpu.make_async_remote_copy(
                    sc_b.at[red, z], sc_b.at[red, flip(z, d)], b_send.at[red, d], b_recv.at[red, d],
                    device_id=(flip(z, d), o), device_id_type=MESH).wait_recv()
            both = jnp.sum(sc_b[red], axis=0)
            for copy in sent:
                copy.wait_send()
            return both

        return finish

    scale = None
    for step in range(STEPS):
        groups = (xa.at[step], xb.at[step])

        def place(d, g, core):
            chip = flip(m, g)
            row = pl.multiple_of((chip % half) * (2 * rows) + core * rows, rows)
            return flip(z, d), row, 2 * chip + core

        sent = []
        counter = [0]

        def send(d, g, core, to_z, to_m, to_core, to_d, to_g):
            sector, row, owner = place(d, g, core)
            source = groups[1 if g >= half else 0].at[sector, pl.ds(row, rows), :]
            target = groups[1 if to_g >= half else 0].at[sector, pl.ds(row, rows), :]
            copy = pltpu.make_async_remote_copy(
                source, target, x_send.at[step, counter[0]], x_recv.at[step, sector, owner],
                device_id=(to_z, 2 * to_m + to_core), device_id_type=MESH)
            counter[0] += 1
            copy.start()
            sent.append(copy)

        def arrive(d, g, core):
            sector, row, owner = place(d, g, core)
            slot = groups[1 if g >= half else 0].at[sector, pl.ds(row, rows), :]
            pltpu.make_async_remote_copy(
                slot, slot, x_send.at[step, 0], x_recv.at[step, sector, owner],
                device_id=(z, flip(o, 1)), device_id_type=MESH).wait_recv()

        own_sector, own_row, own_place = place(0, 0, c)
        groups[0][own_sector, pl.ds(own_row, rows), :] = cur[...].astype(BF16)

        def spread(d, g):
            if d == 0 and g == 0:
                for other in range(1, sectors):
                    send(0, 0, c, flip(z, other), m, c, other, 0)
            else:
                arrive(d, g, c)
            order = list(range(bits)) if d < sectors // 2 else list(range(bits))[::-1]
            last = -1
            for at, bit in enumerate(order):
                if g & (1 << bit):
                    last = at
            for bit in order[last + 1 :]:
                send(d, g, c, z, flip(m, 1 << bit), c, d, g ^ (1 << bit))
            send(d, g, c, z, m, 1 - c, d, g)

        plan = [(d, g) for d in range(sectors) for g in range(chips)]
        level = lambda g: bin(g).count("1")
        plan.sort(key=lambda dg: (dg[1] >= half and level(dg[1]) > 1, dg[0] + level(dg[1]), level(dg[1]), dg))
        early = [dg for dg in plan if not (dg[1] >= half and level(dg[1]) > 1)]
        late = [dg for dg in plan if dg not in early]

        def rotate(group, at):
            first = pl.multiple_of(at * half_rows, half_rows)
            for p in range(pairs):
                x = group[coup[z, o * pairs + p]]
                t = lax.dot_general(x, rv[p], (((1,), (1,)), ((), ())), preferred_element_type=F32)
                tt[p, pl.ds(first, half_rows), :] = t.astype(BF16)

        for d, g in early:
            spread(d, g)
        for d in range(sectors):
            for g in range(half):
                arrive(d, g, 1 - c)
        if step == 0:
            loads[0].wait()
        rotate(groups[0], top)
        for d, g in late:
            spread(d, g)
        for d in range(sectors):
            for g in range(half, chips):
                arrive(d, g, 1 - c)
        rotate(groups[1], 1 - top)
        if step == 0:
            loads[1].wait()

        pieces = []

        def r1(g):
            return pltpu.make_async_remote_copy(
                s1_tx.at[step, g], s1_rx.at[step, g], r1_send.at[step, g], r1_recv.at[step, g],
                device_id=(z, 2 * m + 1 - c), device_id_type=MESH)

        def r2(g):
            return pltpu.make_async_remote_copy(
                s2_tx.at[step, g], s2_rx.at[step, g], r2_send.at[step, g], r2_recv.at[step, g],
                device_id=(z, 2 * flip(m, g) + c), device_id_type=MESH)

        def block(which, g, core):
            row = pl.multiple_of((flip(m, g) % half) * (2 * rows) + core * rows, rows)
            return acc[which, pl.ds(row, rows), :]

        numer = None
        for which in (1, 0):
            at = top if which == 0 else 1 - top
            first = pl.multiple_of(at * half_rows, half_rows)
            total = None
            for p in range(pairs):
                part = jnp.dot(lv[p, pl.ds(first, half_rows), :], tt[p], preferred_element_type=F32)
                total = part if total is None else total + part
            acc[which] = total
            for g in reversed(range(which * half, which * half + half)):
                s1_tx[step, g] = block(which, g, 1 - c).astype(BF16)
                r1(g).start()
            tile = folded(groups[which][z].astype(F32) * acc[which])
            numer = tile if numer is None else numer + tile
        sc_t[step, 0] = numer
        sc_t[step, 1] = folded(cur[...] * cur[...])
        finish = reduce_tile(step)
        for g in reversed(range(1, chips)):
            r1(g).wait_recv()
            s2_tx[step, g] = (
                block(1 if g >= half else 0, g, c) + s1_rx[step, g].astype(F32)
            ).astype(BF16)
            r2(g).start()
        both = finish()
        r1(0).wait_recv()
        sigma = block(0, 0, c) + s1_rx[step, 0].astype(F32)
        for g in range(1, chips):
            r2(g).wait_recv()
            sigma = sigma + s2_rx[step, g].astype(F32)
        sigma = sigma * mask
        numer, denom = total_of(both[0]), total_of(both[1])
        if step == 0:
            theta = numer / (denom + 1e-06)
        else:
            scale = lax.rsqrt(denom / entry_total + 1e-06)
            theta = (scale * scale * numer) / (scale * scale * denom + 1e-06)
        energies[step] = theta[0, 0]
        gap = diag[...] - theta
        held = cur[...]
        update = held - (sigma - theta * held) * (gap / (gap * gap + 1.0))
        if step > 0:
            update = update * scale
        cur[...] = update
        for copy in sent:
            copy.wait_send()
        for g in range(chips):
            r1(g).wait_send()
        for g in range(1, chips):
            r2(g).wait_send()

    sc_t[STEPS, 0] = folded(cur[...] * cur[...])
    sc_t[STEPS, 1] = jnp.zeros((8, 128), F32)
    squares = total_of(reduce_tile(STEPS)()[0])
    vec[...] = cur[...] * lax.rsqrt(squares / entry_total + 1e-06)


def shards(sectors, ops, wavefunction, diagonal, left_blocks, right_blocks, coupling, sector_sizes):
    _, rows, width = wavefunction.shape
    pairs = left_blocks.shape[0]
    chips = ops // 2
    half_rows = ops * rows // 2
    entry_total = float(wavefunction.size * sectors * ops)
    vmem = pl.BlockSpec(memory_space=pltpu.VMEM)
    smem = pl.BlockSpec(memory_space=pltpu.SMEM)
    hbm = pl.BlockSpec(memory_space=pl.ANY)
    dma = pltpu.SemaphoreType.DMA
    sends = sectors * ops
    vector, energies = pl.pallas_call(
        functools.partial(kernel, sectors, ops, entry_total),
        out_shape=(
            jax.ShapeDtypeStruct((rows, width), F32),
            jax.ShapeDtypeStruct((STEPS,), F32),
        ),
        in_specs=[smem, smem, vmem, vmem, hbm, hbm],
        out_specs=(vmem, smem),
        scratch_shapes=[
            pltpu.VMEM(left_blocks.shape, BF16),
            pltpu.VMEM(right_blocks.shape, BF16),
            pltpu.VMEM((STEPS, sectors, half_rows, width), BF16),
            pltpu.VMEM((STEPS, sectors, half_rows, width), BF16),
            pltpu.VMEM((pairs, 2 * half_rows, width), BF16),
            pltpu.VMEM((2, half_rows, width), F32),
            pltpu.VMEM((rows, width), F32),
            pltpu.VMEM((STEPS, chips, rows, width), BF16),
            pltpu.VMEM((STEPS, chips, rows, width), BF16),
            pltpu.VMEM((STEPS, chips, rows, width), BF16),
            pltpu.VMEM((STEPS, chips, rows, width), BF16),
            pltpu.VMEM((STEPS + 1, ops, 2, 8, 128), F32),
            pltpu.VMEM((STEPS + 1, sectors, 2, 8, 128), F32),
            pltpu.VMEM((STEPS + 1, 2, 8, 128), F32),
            dma((2,)),
            dma((STEPS, sends)),
            dma((STEPS, sectors, ops)),
            dma((STEPS, chips)),
            dma((STEPS, chips)),
            dma((STEPS, chips)),
            dma((STEPS, chips)),
            dma((STEPS + 1, ops)),
            dma((STEPS + 1, ops)),
            dma((STEPS + 1, sectors)),
            dma((STEPS + 1, sectors)),
        ],
        compiler_params=pltpu.CompilerParams(
            collective_id=0, has_side_effects=True, vmem_limit_bytes=48 * 1024 * 1024
        ),
    )(coupling, sector_sizes, wavefunction[0], diagonal[0], left_blocks, right_blocks)
    return vector[None], energies


def solution(mesh):
    in_specs = (
        P("sector", "op", None),
        P("sector", "op", None),
        P("op", None, None),
        P("op", None, None),
        P(),
        P(),
    )
    out_specs = (P("sector", "op", None), P())
    body = functools.partial(shards, mesh.shape["sector"], mesh.shape["op"])
    return jax.shard_map(body, mesh=mesh, in_specs=in_specs, out_specs=out_specs, check_vma=False)
```

time: 383 us -> 79.2 us (0.21)
  blocking collectives: 193 us -> 0 us
  waiting for transfers between devices: 130 us -> 0 us
  Pallas kernels: 0 us -> 71.8 us
  matrix products: 20.9 us -> 0 us
  between operations: 17.8 us -> 0.65 us
  other arithmetic: 10.7 us -> 0 us
    psum x4 -> x0, blocking collectives: 162 us -> none  [the longest x2 82.7 us: shards(): squares = lax.psum(jnp.sum(update * update), ('sector', 'op'))]
    reduce_scatter x2 -> x0, waiting for transfers between devices: 72.3 us -> none  [shards(): lax.psum_scatter(partial_terms, 'op', scatter_dimension=1, tiled=True)]
    pallas_call x0 -> x1, Pallas kernels: none -> 71.8 us  [shards(): pl.pallas_call(functools.partial(kernel, sectors, ops, entry_total), out_...]
    all_gather x2 -> x0, waiting for transfers between devices: 57.2 us -> none  [shards(): whole = lax.all_gather(rows_all, 'op', axis=1, tiled=True)]
    all_gather x2 -> x0, blocking collectives: 30.9 us -> none  [shards(): rows_all = lax.all_gather(current_low, 'sector', axis=0, tiled=True)]
    dot_general x2 -> x0, matrix products: 20.9 us -> none  [shards(): jnp.einsum('abik,blk->ail', half, right_blocks, preferred_element_type=jn...]
    gather x2 -> x0, local copies, waits for them, and re-layouts: 8.66 us -> none  [shards(): sources = jnp.take(whole, wanted.reshape(-1), axis=0)]
    unnamed x4 -> x12, local copies, waits for them, and re-layouts: 0.01 us -> 6.49 us
  transfers between devices with their start and end apart: 4 -> 0, of which waited for: 4 -> 0; matrix products, arithmetic and copies ran while one was open for 0% -> 0% of each run, Pallas kernels for 0% -> 0%
where the time goes in v1:
time: 79.2 us; the launch traced here: 79 us
  Pallas kernels  71.8 us (91%)
  local copies, waits for them, and re-layouts  6.49 us (8%)
    pallas_call x1, Pallas kernels, shards(): pl.pallas_call(functools.partial(kernel, sectors, ops, entry_total), out_...  71.8 us
    unnamed x12, local copies, waits for them, and re-layouts  6.49 us

profile of v1, /device:TPU:0, one launch (start us, length us, event | category | flops | bytes accessed | tf_op | source)
XLA Modules:
  0.0 79.0 jit_solution(153952100443935337)
XLA Ops:
  0.6 0.0 copy-start
  0.6 2.2 %copy-done = bf16[8,512,512]{2,1,0:T(8,128)(2,1)S(1)} copy-done((bf16[8,512,512]{2,1,0:T(8,128)(2,1)S(1)}, bf16[8,512,512]{2,1,0:T(8,128)(2,1)}, u32[]{:S(2)}) %copy-start) | copy-done | bytes 4194328
  2.8 0.0 copy-start.1
  2.8 0.9 %copy-done.1 = f32[1,64,512]{2,1,0:T(8,128)S(1)} copy-done((f32[1,64,512]{2,1,0:T(8,128)S(1)}, f32[1,64,512]{2,1,0:T(8,128)}, u32[]{:S(2)}) %copy-start.1) | copy-done | bytes 131096
  3.7 0.0 copy-start.2
  3.7 0.9 %copy-done.2 = f32[1,64,512]{2,1,0:T(8,128)S(1)} copy-done((f32[1,64,512]{2,1,0:T(8,128)S(1)}, f32[1,64,512]{2,1,0:T(8,128)}, u32[]{:S(2)}) %copy-start.2) | copy-done | bytes 131096
  4.6 0.0 copy-start.3
  4.6 0.7 copy-done.3
  5.3 0.0 copy-start.4
  5.3 0.7 copy-done.4
  6.0 71.8 %shard_map.77 = (f32[64,512]{1,0:T(8,128)S(1)}, f32[2]{0:T(128)S(1)}) custom-call(s32[4,64]{1,0:T(4,128)S(1)} %copy-done.3, s32[4]{0:T(128)S(1)} %copy-done.4, f32[64,512]{1,0:T(8,128)S(1)} %bitcast.3, f32[64,512]{1,0:T(8,128)S(1)} %bitcast.4, bf16[8,512,512]{2,1,0:T(8,128)(2,1)S(1)} %copy-done, bf16[8,512,512]{2,1,0:T(8,128)(2,1)} %right.1), custom_call_target="tpu_custom_call" | custom-call | tf_op jit(solution)/shard_map/pallas_call | solution.py:270
  77.8 0.7 copy.10
  78.5 0.5 copy.11
Async XLA Ops:
  0.6 2.2 %copy-start = (bf16[8,512,512]{2,1,0:T(8,128)(2,1)S(1)}, bf16[8,512,512]{2,1,0:T(8,128)(2,1)}, u32[]{:S(2)}) copy-start(bf16[8,512,512]{2,1,0:T(8,128)(2,1)} %left.1) | copy-start | bytes 12582916
  2.8 0.9 %copy-start.1 = (f32[1,64,512]{2,1,0:T(8,128)S(1)}, f32[1,64,512]{2,1,0:T(8,128)}, u32[]{:S(2)}) copy-start(f32[1,64,512]{2,1,0:T(8,128)} %param.6) | copy-start | bytes 393220
  3.7 0.9 %copy-start.2 = (f32[1,64,512]{2,1,0:T(8,128)S(1)}, f32[1,64,512]{2,1,0:T(8,128)}, u32[]{:S(2)}) copy-start(f32[1,64,512]{2,1,0:T(8,128)} %param.7) | copy-start | bytes 393220
  4.6 0.7 copy-start.3
  5.3 0.7 copy-start.4

commit v2 on v1

--- a/solution.py
+++ b/solution.py
@@ -37,9 +37,9 @@
 
 def kernel(
     sectors, ops, entry_total,
-    coup, sizes, wf, diag, left, right,
+    coup_in, sizes_in, wf_in, diag_in, left, right,
     vec, energies,
-    lv, rv, xa, xb, tt, acc, cur, s1_tx, s1_rx, s2_tx, s2_rx, sc_a, sc_b, sc_t,
+    coup, sizes, wf, diag, lv, rv, xa, xb, tt, acc, cur, s1_tx, s1_rx, s2_tx, s2_rx, sc_a, sc_b, sc_t,
     load_sem, x_send, x_recv, r1_send, r1_recv, r2_send, r2_recv, a_send, a_recv, b_send, b_recv,
 ):
     rows, width = wf.shape
@@ -53,11 +53,15 @@
     m, c = o // 2, o % 2
     top = m // half
 
-    loads = [
-        pltpu.make_async_copy(right, rv, load_sem.at[0]),
-        pltpu.make_async_copy(left, lv, load_sem.at[1]),
+    small = [(wf_in, wf), (sizes_in, sizes), (coup_in, coup), (diag_in, diag)]
+    small = [
+        pltpu.make_async_copy(src, dst, load_sem.at[at]) for at, (src, dst) in enumerate(small)
     ]
-    for load in loads:
+    loads = [pltpu.make_async_copy(right, rv, load_sem.at[4])] + [
+        pltpu.make_async_copy(left.at[p], lv.at[:, pl.ds(p * width, width)], load_sem.at[5 + p])
+        for p in range(pairs)
+    ]
+    for load in small:
         load.start()
 
     barrier = pltpu.get_barrier_semaphore()
@@ -66,6 +70,10 @@
     for d in range(1, sectors):
         pl.semaphore_signal(barrier, inc=1, device_id=(flip(z, d), o), device_id_type=MESH)
 
+    for load in loads:
+        load.start()
+    small[0].wait()
+    small[1].wait()
     bound = sizes[z]
     row_ids = o * rows + lax.broadcasted_iota(jnp.int32, (rows, width), 0)
     col_ids = lax.broadcasted_iota(jnp.int32, (rows, width), 1)
@@ -110,81 +118,93 @@
     for step in range(STEPS):
         groups = (xa.at[step], xb.at[step])
 
-        def place(d, g, core):
+        def place(r, g, core):
             chip = flip(m, g)
             row = pl.multiple_of((chip % half) * (2 * rows) + core * rows, rows)
-            return flip(z, d), row, 2 * chip + core
+            return z + r, row, 2 * chip + core
 
         sent = []
-        counter = [0]
-
-        def send(d, g, core, to_z, to_m, to_core, to_d, to_g):
-            sector, row, owner = place(d, g, core)
-            source = groups[1 if g >= half else 0].at[sector, pl.ds(row, rows), :]
-            target = groups[1 if to_g >= half else 0].at[sector, pl.ds(row, rows), :]
-            copy = pltpu.make_async_remote_copy(
-                source, target, x_send.at[step, counter[0]], x_recv.at[step, sector, owner],
-                device_id=(to_z, 2 * to_m + to_core), device_id_type=MESH)
-            counter[0] += 1
-            copy.start()
-            sent.append(copy)
-
-        def arrive(d, g, core):
-            sector, row, owner = place(d, g, core)
+
+        def inside(r):
+            return jnp.logical_and(z + r >= 0, z + r < sectors)
+
+        def send(pred, r, g, to_z, to_m, to_core, to_g):
+            at = len(sent)
+
+            def copy():
+                sector, row, owner = place(r, g, c)
+                source = groups[1 if g >= half else 0].at[sector, pl.ds(row, rows), :]
+                target = groups[1 if to_g >= half else 0].at[sector, pl.ds(row, rows), :]
+                return pltpu.make_async_remote_copy(
+                    source, target, x_send.at[at], x_recv.at[step, sector, owner],
+                    device_id=(to_z, 2 * to_m + to_core), device_id_type=MESH)
+
+            sent.append((pred, copy))
+            pl.when(pred)(lambda: copy().start())
+
+        def arrive(r, g, core):
+            sector, row, owner = place(r, g, core)
             slot = groups[1 if g >= half else 0].at[sector, pl.ds(row, rows), :]
             pltpu.make_async_remote_copy(
-                slot, slot, x_send.at[step, 0], x_recv.at[step, sector, owner],
+                slot, slot, x_send.at[0], x_recv.at[step, sector, owner],
                 device_id=(z, flip(o, 1)), device_id_type=MESH).wait_recv()
 
-        own_sector, own_row, own_place = place(0, 0, c)
+        own_sector, own_row, _ = place(0, 0, c)
         groups[0][own_sector, pl.ds(own_row, rows), :] = cur[...].astype(BF16)
 
-        def spread(d, g):
-            if d == 0 and g == 0:
-                for other in range(1, sectors):
-                    send(0, 0, c, flip(z, other), m, c, other, 0)
-            else:
-                arrive(d, g, c)
-            order = list(range(bits)) if d < sectors // 2 else list(range(bits))[::-1]
+        def spread(r, g):
+            here = inside(r)
+            if r or g:
+                pl.when(here)(lambda: arrive(r, g, c))
+            if g == 0 and r <= 0:
+                send(jnp.logical_and(here, z + 1 < sectors), r, 0, z + 1, m, c, 0)
+            if g == 0 and r >= 0:
+                send(jnp.logical_and(here, z >= 1), r, 0, z - 1, m, c, 0)
+            order = list(range(bits)) if r % 2 == 0 else list(range(bits))[::-1]
             last = -1
             for at, bit in enumerate(order):
                 if g & (1 << bit):
                     last = at
             for bit in order[last + 1 :]:
-                send(d, g, c, z, flip(m, 1 << bit), c, d, g ^ (1 << bit))
-            send(d, g, c, z, m, 1 - c, d, g)
-
-        plan = [(d, g) for d in range(sectors) for g in range(chips)]
+                send(here, r, g, z, flip(m, 1 << bit), c, g ^ (1 << bit))
+            send(here, r, g, z, m, 1 - c, g)
+
+        def arrive_sibling(first, end):
+            for r in range(1 - sectors, sectors):
+
+                @pl.when(inside(r))
+                def _():
+                    for g in range(first, end):
+                        arrive(r, g, 1 - c)
+
         level = lambda g: bin(g).count("1")
-        plan.sort(key=lambda dg: (dg[1] >= half and level(dg[1]) > 1, dg[0] + level(dg[1]), level(dg[1]), dg))
-        early = [dg for dg in plan if not (dg[1] >= half and level(dg[1]) > 1)]
-        late = [dg for dg in plan if dg not in early]
+        is_late = lambda rg: rg[1] >= half and level(rg[1]) > 1
+        plan = [(r, g) for r in range(1 - sectors, sectors) for g in range(chips)]
+        plan.sort(key=lambda rg: (is_late(rg), abs(rg[0]) + level(rg[1]), level(rg[1]), abs(rg[0]), rg))
+        early = [rg for rg in plan if not is_late(rg)]
+        late = [rg for rg in plan if is_late(rg)]
 
         def rotate(group, at):
             first = pl.multiple_of(at * half_rows, half_rows)
             for p in range(pairs):
                 x = group[coup[z, o * pairs + p]]
                 t = lax.dot_general(x, rv[p], (((1,), (1,)), ((), ())), preferred_element_type=F32)
-                tt[p, pl.ds(first, half_rows), :] = t.astype(BF16)
-
-        for d, g in early:
-            spread(d, g)
-        for d in range(sectors):
-            for g in range(half):
-                arrive(d, g, 1 - c)
+                tt[pl.ds(pl.multiple_of(p * width + first, half_rows), half_rows), :] = t.astype(BF16)
+
+        for r, g in early:
+            spread(r, g)
+        arrive_sibling(0, half)
         if step == 0:
+            small[2].wait()
             loads[0].wait()
         rotate(groups[0], top)
-        for d, g in late:
-            spread(d, g)
-        for d in range(sectors):
-            for g in range(half, chips):
-                arrive(d, g, 1 - c)
+        for r, g in late:
+            spread(r, g)
+        arrive_sibling(half, chips)
         rotate(groups[1], 1 - top)
         if step == 0:
-            loads[1].wait()
-
-        pieces = []
+            for load in loads[1:] + small[3:]:
+                load.wait()
 
         def r1(g):
             return pltpu.make_async_remote_copy(
@@ -200,29 +220,33 @@
             row = pl.multiple_of((flip(m, g) % half) * (2 * rows) + core * rows, rows)
             return acc[which, pl.ds(row, rows), :]
 
-        numer = None
-        for which in (1, 0):
+        def partial(which, column, end):
             at = top if which == 0 else 1 - top
             first = pl.multiple_of(at * half_rows, half_rows)
-            total = None
-            for p in range(pairs):
-                part = jnp.dot(lv[p, pl.ds(first, half_rows), :], tt[p], preferred_element_type=F32)
-                total = part if total is None else total + part
-            acc[which] = total
+            acc[which, :, column:end] = jnp.dot(
+                lv[pl.ds(first, half_rows), :], tt[:, column:end], preferred_element_type=F32)
+
+        def to_sibling(which):
             for g in reversed(range(which * half, which * half + half)):
                 s1_tx[step, g] = block(which, g, 1 - c).astype(BF16)
                 r1(g).start()
-            tile = folded(groups[which][z].astype(F32) * acc[which])
-            numer = tile if numer is None else numer + tile
-        sc_t[step, 0] = numer
+
+        def to_chips(which):
+            for g in reversed(range(max(1, which * half), which * half + half)):
+                r1(g).wait_recv()
+                s2_tx[step, g] = (block(which, g, c) + s1_rx[step, g].astype(F32)).astype(BF16)
+                r2(g).start()
+
+        partial(1, 0, width)
+        to_sibling(1)
+        partial(0, 0, width // 2)
+        to_chips(1)
+        partial(0, width // 2, width)
+        to_sibling(0)
+        sc_t[step, 0] = folded(xa[step, z].astype(F32) * acc[0]) + folded(xb[step, z].astype(F32) * acc[1])
         sc_t[step, 1] = folded(cur[...] * cur[...])
         finish = reduce_tile(step)
-        for g in reversed(range(1, chips)):
-            r1(g).wait_recv()
-            s2_tx[step, g] = (
-                block(1 if g >= half else 0, g, c) + s1_rx[step, g].astype(F32)
-            ).astype(BF16)
-            r2(g).start()
+        to_chips(0)
         both = finish()
         r1(0).wait_recv()
         sigma = block(0, 0, c) + s1_rx[step, 0].astype(F32)
@@ -243,8 +267,8 @@
         if step > 0:
             update = update * scale
         cur[...] = update
-        for copy in sent:
-            copy.wait_send()
+        for pred, copy in sent:
+            pl.when(pred)(lambda copy=copy: copy().wait_send())
         for g in range(chips):
             r1(g).wait_send()
         for g in range(1, chips):
@@ -266,21 +290,25 @@
     smem = pl.BlockSpec(memory_space=pltpu.SMEM)
     hbm = pl.BlockSpec(memory_space=pl.ANY)
     dma = pltpu.SemaphoreType.DMA
-    sends = sectors * ops
+    sends = (2 * sectors - 1) * 2 * chips + 2
     vector, energies = pl.pallas_call(
         functools.partial(kernel, sectors, ops, entry_total),
         out_shape=(
             jax.ShapeDtypeStruct((rows, width), F32),
             jax.ShapeDtypeStruct((STEPS,), F32),
         ),
-        in_specs=[smem, smem, vmem, vmem, hbm, hbm],
+        in_specs=[hbm] * 6,
         out_specs=(vmem, smem),
         scratch_shapes=[
-            pltpu.VMEM(left_blocks.shape, BF16),
+            pltpu.SMEM(coupling.shape, jnp.int32),
+            pltpu.SMEM(sector_sizes.shape, jnp.int32),
+            pltpu.VMEM((rows, width), F32),
+            pltpu.VMEM((rows, width), F32),
+            pltpu.VMEM((width, pairs * width), BF16),
             pltpu.VMEM(right_blocks.shape, BF16),
             pltpu.VMEM((STEPS, sectors, half_rows, width), BF16),
             pltpu.VMEM((STEPS, sectors, half_rows, width), BF16),
-            pltpu.VMEM((pairs, 2 * half_rows, width), BF16),
+            pltpu.VMEM((pairs * width, width), BF16),
             pltpu.VMEM((2, half_rows, width), F32),
             pltpu.VMEM((rows, width), F32),
             pltpu.VMEM((STEPS, chips, rows, width), BF16),
@@ -290,8 +318,8 @@
             pltpu.VMEM((STEPS + 1, ops, 2, 8, 128), F32),
             pltpu.VMEM((STEPS + 1, sectors, 2, 8, 128), F32),
             pltpu.VMEM((STEPS + 1, 2, 8, 128), F32),
-            dma((2,)),
-            dma((STEPS, sends)),
+            dma((5 + pairs,)),
+            dma((sends,)),
             dma((STEPS, sectors, ops)),
             dma((STEPS, chips)),
             dma((STEPS, chips)),
@@ -303,7 +331,7 @@
             dma((STEPS + 1, sectors)),
         ],
         compiler_params=pltpu.CompilerParams(
-            collective_id=0, has_side_effects=True, vmem_limit_bytes=48 * 1024 * 1024
+            collective_id=0, has_side_effects=True, vmem_limit_bytes=62 * 1024 * 1024
         ),
     )(coupling, sector_sizes, wavefunction[0], diagonal[0], left_blocks, right_blocks)
     return vector[None], energies

time: 79.2 us -> 81.1 us (1.024)
  Pallas kernels: 71.8 us -> 77.5 us
  local copies, waits for them, and re-layouts: 6.49 us -> 2.74 us
    pallas_call x1, Pallas kernels: 71.8 us -> 77.5 us  [shards(): pl.pallas_call(functools.partial(kernel, sectors, ops, entry_total), out_...]
    unnamed x12 -> x2, local copies, waits for them, and re-layouts: 6.49 us -> 2.74 us
where the time goes in v2:
time: 81.1 us; the launch traced here: 80.9 us
  Pallas kernels  77.5 us (96%)
  local copies, waits for them, and re-layouts  2.74 us (3%)
    pallas_call x1, Pallas kernels, shards(): pl.pallas_call(functools.partial(kernel, sectors, ops, entry_total), out_...  77.5 us
    unnamed x2, local copies, waits for them, and re-layouts  2.74 us

profile of v2, /device:TPU:0, one launch (start us, length us, event | category | flops | bytes accessed | tf_op | source)
XLA Modules:
  0.0 80.9 jit_solution(15364086591957845353)
XLA Ops:
  0.6 77.5 %shard_map.77 = (f32[64,512]{1,0:T(8,128)}, f32[2]{0:T(128)}) custom-call(s32[4,64]{1,0:T(4,128)} %coup_in.1, s32[4]{0:T(128)} %sizes_in.1, f32[64,512]{1,0:T(8,128)} %bitcast.3, f32[64,512]{1,0:T(8,128)} %bitcast.4, bf16[8,512,512]{2,1,0:T(8,128)(2,1)} %left.1, bf16[8,512,512]{2,1,0:T(8,128)(2,1)} %right.1), custom_call_target="tpu_custom_call" | custom-call | tf_op jit(solution)/shard_map/pallas_call | solution.py:294
  78.2 1.6 %copy.10 = f32[1,64,512]{2,1,0:T(8,128)} copy(f32[1,64,512]{2,1,0:T(8,128)} %bitcast.5) | data formatting | bytes 262144
  79.7 1.2 %copy.11 = f32[2]{0:T(128)} copy(f32[2]{0:T(128)} %get-tuple-element.9) | data formatting | bytes 16

commit v3 on v2

v3 whole, which is shorter than its diff:
```python
import functools

import jax
import jax.numpy as jnp
from jax import lax
from jax.experimental import pallas as pl
from jax.experimental.pallas import tpu as pltpu
from jax.sharding import PartitionSpec as P

STEPS = 2
MESH = pl.DeviceIdType.MESH
F32 = jnp.float32
BF16 = jnp.bfloat16


def flip(value, mask):
    bit = 1
    while bit <= mask:
        if mask & bit:
            value = value + bit - 2 * bit * ((value // bit) % 2)
        bit *= 2
    return value


def folded(x):
    rows, width = x.shape
    x = jnp.sum(x.reshape(rows // 8, 8, width), axis=0)
    total = x[:, 0:128]
    for at in range(128, width, 128):
        total = total + x[:, at : at + 128]
    return total


def total_of(tile):
    return jnp.sum(jnp.sum(tile, axis=0, keepdims=True), axis=1, keepdims=True)


def kernel(
    sectors, ops, entry_total,
    coup_in, sizes_in, wf_in, diag_in, left, right,
    vec, energies,
    coup, sizes, wf, diag, lv, rv, xa, xb, tt, acc, cur, s1_tx, s1_rx, s2_tx, s2_rx, sc_a, sc_b, sc_t,
    load_sem, x_send, x_recv, r1_send, r1_recv, r2_send, r2_recv, a_send, a_recv, b_send, b_recv,
):
    rows, width = wf.shape
    pairs = left.shape[0]
    chips = ops // 2
    half = chips // 2
    bits = chips.bit_length() - 1
    half_rows = half * 2 * rows
    z = lax.axis_index("sector")
    o = lax.axis_index("op")
    m, c = o // 2, o % 2
    top = m // half
    chip_at = [flip(m, g) for g in range(chips)]
    op_at = [flip(o, k) for k in range(ops)]
    z_at = [flip(z, d) for d in range(sectors)]
    row_at = [
        [pl.multiple_of((chip_at[g] % half) * (2 * rows) + core * rows, rows) for core in (c, 1 - c)]
        for g in range(chips)
    ]
    first_at = [pl.multiple_of(at * half_rows, half_rows) for at in (top, 1 - top)]

    small = [(wf_in, wf), (sizes_in, sizes), (coup_in, coup), (diag_in, diag)]
    small = [
        pltpu.make_async_copy(src, dst, load_sem.at[at]) for at, (src, dst) in enumerate(small)
    ]
    loads = [pltpu.make_async_copy(right, rv, load_sem.at[4])] + [
        pltpu.make_async_copy(left.at[p], lv.at[:, pl.ds(p * width, width)], load_sem.at[5 + p])
        for p in range(pairs)
    ]
    for load in small:
        load.start()

    barrier = pltpu.get_barrier_semaphore()
    for k in range(1, ops):
        pl.semaphore_signal(barrier, inc=1, device_id=(z, op_at[k]), device_id_type=MESH)
    for d in range(1, sectors):
        pl.semaphore_signal(barrier, inc=1, device_id=(z_at[d], o), device_id_type=MESH)

    for load in loads:
        load.start()
    small[0].wait()
    small[1].wait()
    bound = sizes[z]
    row_ids = o * rows + lax.broadcasted_iota(jnp.int32, (rows, width), 0)
    col_ids = lax.broadcasted_iota(jnp.int32, (rows, width), 1)
    mask = ((row_ids < bound) & (col_ids < bound)).astype(F32)
    cur[...] = wf[...] * mask
    pl.semaphore_wait(barrier, ops - 1 + sectors - 1)

    def reduce_tile(red):
        sent = []
        for k in range(1, ops):
            copy = pltpu.make_async_remote_copy(
                sc_t.at[red], sc_a.at[red, o], a_send.at[red, k], a_recv.at[red, k],
                device_id=(z, op_at[k]), device_id_type=MESH)
            copy.start()
            sent.append(copy)
        sc_a[red, o] = sc_t[red]

        def finish():
            for k in range(1, ops):
                pltpu.make_async_remote_copy(
                    sc_t.at[red], sc_a.at[red, op_at[k]], a_send.at[red, k], a_recv.at[red, k],
                    device_id=(z, op_at[k]), device_id_type=MESH).wait_recv()
            sc_b[red, z] = jnp.sum(sc_a[red], axis=0)
            for d in range(1, sectors):
                copy = pltpu.make_async_remote_copy(
                    sc_b.at[red, z], sc_b.at[red, z], b_send.at[red, d], b_recv.at[red, d],
                    device_id=(z_at[d], o), device_id_type=MESH)
                copy.start()
                sent.append(copy)
            for d in range(1, sectors):
                pltpu.make_async_remote_copy(
                    sc_b.at[red, z], sc_b.at[red, z_at[d]], b_send.at[red, d], b_recv.at[red, d],
                    device_id=(z_at[d], o), device_id_type=MESH).wait_recv()
            both = jnp.sum(sc_b[red], axis=0)
            for copy in sent:
                copy.wait_send()
            return both

        return finish

    scale = None
    for step in range(STEPS):
        groups = (xa.at[step], xb.at[step])

        sent = []

        def slot(d, g, other):
            first = (2 * (g % half) + other) * rows
            return groups[1 if g >= half else 0].at[d, pl.ds(first, rows), :]

        def send(d, g, to, to_d, to_g, other):
            copy = pltpu.make_async_remote_copy(
                slot(d, g, 0), slot(to_d, to_g, other),
                x_send.at[step, len(sent)], x_recv.at[step, to_d, to_g, other],
                device_id=to, device_id_type=MESH)
            copy.start()
            sent.append(copy)

        def arrive(d, g, other):
            here = slot(d, g, other)
            pltpu.make_async_remote_copy(
                here, here, x_send.at[step, 0], x_recv.at[step, d, g, other],
                device_id=(z, op_at[1]), device_id_type=MESH).wait_recv()

        groups[0][0, 0:rows, :] = cur[...].astype(BF16)

        def spread(d, g):
            if d or g:
                arrive(d, g, 0)
            order = list(range(bits)) if d % 2 == 0 else list(range(bits))[::-1]
            last = -1
            for at, bit in enumerate(order):
                if g & (1 << bit):
                    last = at
            if d == 0 and g == 0 and sectors > 1:
                send(0, 0, (z_at[1], o), 1, 0, 0)
            for bit in order[last + 1 :]:
                send(d, g, (z, op_at[2 << bit]), d, g ^ (1 << bit), 0)
            if d == 0 and g == 0:
                for far in range(2, sectors):
                    send(0, 0, (z_at[far], o), far, 0, 0)
            send(d, g, (z, op_at[1]), d, g, 1)

        level = lambda g: bin(g).count("1")
        is_late = lambda dg: dg[1] >= half and level(dg[1]) > 1
        plan = [(d, g) for d in range(sectors) for g in range(chips)]
        plan.sort(key=lambda dg: (is_late(dg), dg[0] + level(dg[1]), dg))
        early = [dg for dg in plan if not is_late(dg)]
        late = [dg for dg in plan if is_late(dg)]

        def rotate(which):
            for p in range(pairs):
                x = groups[which][coup[z, o * pairs + p] ^ z]
                t = lax.dot_general(x, rv[p], (((1,), (1,)), ((), ())), preferred_element_type=F32)
                t = t.astype(BF16)
                for g in range(half):
                    for other in range(2):
                        row = pl.multiple_of(p * width + first_at[which] + row_at[g + which * half][other], rows)
                        first = (2 * g + other) * rows
                        tt[pl.ds(row, rows), :] = t[first : first + rows]

        def arrive_sibling(first, end):
            for d in range(sectors):
                for g in range(first, end):
                    arrive(d, g, 1)

        for d, g in early:
            spread(d, g)
        arrive_sibling(0, half)
        if step == 0:
            small[2].wait()
            loads[0].wait()
        rotate(0)
        for d, g in late:
            spread(d, g)
        arrive_sibling(half, chips)
        rotate(1)
        if step == 0:
            for load in loads[1:] + small[3:]:
                load.wait()

        def r1(g):
            return pltpu.make_async_remote_copy(
                s1_tx.at[step, g], s1_rx.at[step, g], r1_send.at[step, g], r1_recv.at[step, g],
                device_id=(z, op_at[1]), device_id_type=MESH)

        def r2(g):
            return pltpu.make_async_remote_copy(
                s2_tx.at[step, g], s2_rx.at[step, g], r2_send.at[step, g], r2_recv.at[step, g],
                device_id=(z, op_at[2 * g]), device_id_type=MESH)

        def block(g, other):
            return acc[1 if g >= half else 0, pl.ds(row_at[g][other], rows), :]

        def inner(g, other):
            return folded(slot(0, g, other)[...].astype(F32) * block(g, other))

        def partial(which, column, end):
            acc[which, :, column:end] = jnp.dot(
                lv[pl.ds(first_at[which], half_rows), :], tt[:, column:end], preferred_element_type=F32)

        def to_sibling(which):
            for g in reversed(range(which * half, which * half + half)):
                s1_tx[step, g] = block(g, 1).astype(BF16)
                r1(g).start()

        def to_chips(which):
            for g in reversed(range(max(1, which * half), which * half + half)):
                r1(g).wait_recv()
                s2_tx[step, g] = (block(g, 0) + s1_rx[step, g].astype(F32)).astype(BF16)
                r2(g).start()

        partial(1, 0, width)
        to_sibling(1)
        partial(0, 0, width // 2)
        to_chips(1)
        partial(0, width // 2, width)
        to_sibling(0)
        sc_t[step, 0] = sum(inner(g, other) for g in range(chips) for other in range(2))
        sc_t[step, 1] = folded(cur[...] * cur[...])
        finish = reduce_tile(step)
        to_chips(0)
        both = finish()
        r1(0).wait_recv()
        sigma = block(0, 0) + s1_rx[step, 0].astype(F32)
        for g in range(1, chips):
            r2(g).wait_recv()
            sigma = sigma + s2_rx[step, g].astype(F32)
        sigma = sigma * mask
        numer, denom = total_of(both[0]), total_of(both[1])
        if step == 0:
            theta = numer / (denom + 1e-06)
        else:
            scale = lax.rsqrt(denom / entry_total + 1e-06)
            theta = (scale * scale * numer) / (scale * scale * denom + 1e-06)
        energies[step] = theta[0, 0]
        gap = diag[...] - theta
        held = cur[...]
        update = held - (sigma - theta * held) * (gap / (gap * gap + 1.0))
        if step > 0:
            update = update * scale
        cur[...] = update
        for copy in sent:
            copy.wait_send()
        for g in range(chips):
            r1(g).wait_send()
        for g in range(1, chips):
            r2(g).wait_send()

    sc_t[STEPS, 0] = folded(cur[...] * cur[...])
    sc_t[STEPS, 1] = jnp.zeros((8, 128), F32)
    squares = total_of(reduce_tile(STEPS)()[0])
    vec[...] = cur[...] * lax.rsqrt(squares / entry_total + 1e-06)


def shards(sectors, ops, wavefunction, diagonal, left_blocks, right_blocks, coupling, sector_sizes):
    _, rows, width = wavefunction.shape
    pairs = left_blocks.shape[0]
    chips = ops // 2
    half_rows = ops * rows // 2
    entry_total = float(wavefunction.size * sectors * ops)
    vmem = pl.BlockSpec(memory_space=pltpu.VMEM)
    smem = pl.BlockSpec(memory_space=pltpu.SMEM)
    hbm = pl.BlockSpec(memory_space=pl.ANY)
    dma = pltpu.SemaphoreType.DMA
    vector, energies = pl.pallas_call(
        functools.partial(kernel, sectors, ops, entry_total),
        out_shape=(
            jax.ShapeDtypeStruct((rows, width), F32),
            jax.ShapeDtypeStruct((STEPS,), F32),
        ),
        in_specs=[hbm] * 6,
        out_specs=(vmem, smem),
        scratch_shapes=[
            pltpu.SMEM(coupling.shape, jnp.int32),
            pltpu.SMEM(sector_sizes.shape, jnp.int32),
            pltpu.VMEM((rows, width), F32),
            pltpu.VMEM((rows, width), F32),
            pltpu.VMEM((width, pairs * width), BF16),
            pltpu.VMEM(right_blocks.shape, BF16),
            pltpu.VMEM((STEPS, sectors, half_rows, width), BF16),
            pltpu.VMEM((STEPS, sectors, half_rows, width), BF16),
            pltpu.VMEM((pairs * width, width), BF16),
            pltpu.VMEM((2, half_rows, width), F32),
            pltpu.VMEM((rows, width), F32),
            pltpu.VMEM((STEPS, chips, rows, width), BF16),
            pltpu.VMEM((STEPS, chips, rows, width), BF16),
            pltpu.VMEM((STEPS, chips, rows, width), BF16),
            pltpu.VMEM((STEPS, chips, rows, width), BF16),
            pltpu.VMEM((STEPS + 1, ops, 2, 8, 128), F32),
            pltpu.VMEM((STEPS + 1, sectors, 2, 8, 128), F32),
            pltpu.VMEM((STEPS + 1, 2, 8, 128), F32),
            dma((5 + pairs,)),
            dma((STEPS, sectors * ops)),
            dma((STEPS, sectors, chips, 2)),
            dma((STEPS, chips)),
            dma((STEPS, chips)),
            dma((STEPS, chips)),
            dma((STEPS, chips)),
            dma((STEPS + 1, ops)),
            dma((STEPS + 1, ops)),
            dma((STEPS + 1, sectors)),
            dma((STEPS + 1, sectors)),
        ],
        compiler_params=pltpu.CompilerParams(
            collective_id=0, has_side_effects=True, vmem_limit_bytes=62 * 1024 * 1024
        ),
    )(coupling, sector_sizes, wavefunction[0], diagonal[0], left_blocks, right_blocks)
    return vector[None], energies


def solution(mesh):
    in_specs = (
        P("sector", "op", None),
        P("sector", "op", None),
        P("op", None, None),
        P("op", None, None),
        P(),
        P(),
    )
    out_specs = (P("sector", "op", None), P())
    body = functools.partial(shards, mesh.shape["sector"], mesh.shape["op"])
    return jax.shard_map(body, mesh=mesh, in_specs=in_specs, out_specs=out_specs, check_vma=False)
```

time: 81.1 us -> 86 us (1.060)
  Pallas kernels: 77.5 us -> 82.5 us
    pallas_call x1, Pallas kernels: 77.5 us -> 82.5 us  [shards(): pl.pallas_call(functools.partial(kernel, sectors, ops, entry_total), out_...]
where the time goes in v3:
time: 86 us; the launch traced here: 85.9 us
  Pallas kernels  82.5 us (96%)
  local copies, waits for them, and re-layouts  2.74 us (3%)
    pallas_call x1, Pallas kernels, shards(): pl.pallas_call(functools.partial(kernel, sectors, ops, entry_total), out_...  82.5 us
    unnamed x2, local copies, waits for them, and re-layouts  2.74 us

profile of v3, /device:TPU:0, one launch (start us, length us, event | category | flops | bytes accessed | tf_op | source)
XLA Modules:
  0.0 85.9 jit_solution(13155224481162106237)
XLA Ops:
  0.6 82.5 %shard_map.77 = (f32[64,512]{1,0:T(8,128)}, f32[2]{0:T(128)}) custom-call(s32[4,64]{1,0:T(4,128)} %coup_in.1, s32[4]{0:T(128)} %sizes_in.1, f32[64,512]{1,0:T(8,128)} %bitcast.3, f32[64,512]{1,0:T(8,128)} %bitcast.4, bf16[8,512,512]{2,1,0:T(8,128)(2,1)} %left.1, bf16[8,512,512]{2,1,0:T(8,128)(2,1)} %right.1), custom_call_target="tpu_custom_call" | custom-call | tf_op jit(solution)/shard_map/pallas_call | solution.py:290
  83.1 1.6 %copy.10 = f32[1,64,512]{2,1,0:T(8,128)} copy(f32[1,64,512]{2,1,0:T(8,128)} %bitcast.5) | data formatting | bytes 262144
  84.7 1.2 %copy.11 = f32[2]{0:T(128)} copy(f32[2]{0:T(128)} %get-tuple-element.9) | data formatting | bytes 16

commit v4 on v3

--- a/solution.py
+++ b/solution.py
@@ -65,9 +65,9 @@
     small = [
         pltpu.make_async_copy(src, dst, load_sem.at[at]) for at, (src, dst) in enumerate(small)
     ]
-    loads = [pltpu.make_async_copy(right, rv, load_sem.at[4])] + [
-        pltpu.make_async_copy(left.at[p], lv.at[:, pl.ds(p * width, width)], load_sem.at[5 + p])
-        for p in range(pairs)
+    loads = [
+        pltpu.make_async_copy(right, rv, load_sem.at[4]),
+        pltpu.make_async_copy(left, lv, load_sem.at[5]),
     ]
     for load in small:
         load.start()
@@ -129,12 +129,12 @@
         sent = []
 
         def slot(d, g, other):
-            first = (2 * (g % half) + other) * rows
-            return groups[1 if g >= half else 0].at[d, pl.ds(first, rows), :]
+            return groups[1 if g >= half else 0].at[d, pl.ds(row_at[g][other], rows), :]
 
         def send(d, g, to, to_d, to_g, other):
             copy = pltpu.make_async_remote_copy(
-                slot(d, g, 0), slot(to_d, to_g, other),
+                slot(d, g, 0),
+                groups[1 if to_g >= half else 0].at[to_d, pl.ds(row_at[g][0], rows), :],
                 x_send.at[step, len(sent)], x_recv.at[step, to_d, to_g, other],
                 device_id=to, device_id_type=MESH)
             copy.start()
@@ -146,7 +146,7 @@
                 here, here, x_send.at[step, 0], x_recv.at[step, d, g, other],
                 device_id=(z, op_at[1]), device_id_type=MESH).wait_recv()
 
-        groups[0][0, 0:rows, :] = cur[...].astype(BF16)
+        groups[0][0, pl.ds(row_at[0][0], rows), :] = cur[...].astype(BF16)
 
         def spread(d, g):
             if d or g:
@@ -176,12 +176,7 @@
             for p in range(pairs):
                 x = groups[which][coup[z, o * pairs + p] ^ z]
                 t = lax.dot_general(x, rv[p], (((1,), (1,)), ((), ())), preferred_element_type=F32)
-                t = t.astype(BF16)
-                for g in range(half):
-                    for other in range(2):
-                        row = pl.multiple_of(p * width + first_at[which] + row_at[g + which * half][other], rows)
-                        first = (2 * g + other) * rows
-                        tt[pl.ds(row, rows), :] = t[first : first + rows]
+                tt[p, pl.ds(first_at[which], half_rows), :] = t.astype(BF16)
 
         def arrive_sibling(first, end):
             for d in range(sectors):
@@ -216,12 +211,13 @@
         def block(g, other):
             return acc[1 if g >= half else 0, pl.ds(row_at[g][other], rows), :]
 
-        def inner(g, other):
-            return folded(slot(0, g, other)[...].astype(F32) * block(g, other))
-
-        def partial(which, column, end):
-            acc[which, :, column:end] = jnp.dot(
-                lv[pl.ds(first_at[which], half_rows), :], tt[:, column:end], preferred_element_type=F32)
+        def partial(which, first, end):
+            total = None
+            for p in range(first, end):
+                part = jnp.dot(
+                    lv[p, pl.ds(first_at[which], half_rows), :], tt[p], preferred_element_type=F32)
+                total = part if total is None else total + part
+            return total
 
         def to_sibling(which):
             for g in reversed(range(which * half, which * half + half)):
@@ -234,13 +230,15 @@
                 s2_tx[step, g] = (block(g, 0) + s1_rx[step, g].astype(F32)).astype(BF16)
                 r2(g).start()
 
-        partial(1, 0, width)
+        acc[1] = partial(1, 0, pairs)
         to_sibling(1)
-        partial(0, 0, width // 2)
+        acc[0] = partial(0, 0, pairs // 2)
         to_chips(1)
-        partial(0, width // 2, width)
+        acc[0] += partial(0, pairs // 2, pairs)
         to_sibling(0)
-        sc_t[step, 0] = sum(inner(g, other) for g in range(chips) for other in range(2))
+        sc_t[step, 0] = (
+            folded(xa[step, 0].astype(F32) * acc[0]) + folded(xb[step, 0].astype(F32) * acc[1])
+        )
         sc_t[step, 1] = folded(cur[...] * cur[...])
         finish = reduce_tile(step)
         to_chips(0)
@@ -300,11 +298,11 @@
             pltpu.SMEM(sector_sizes.shape, jnp.int32),
             pltpu.VMEM((rows, width), F32),
             pltpu.VMEM((rows, width), F32),
-            pltpu.VMEM((width, pairs * width), BF16),
+            pltpu.VMEM(left_blocks.shape, BF16),
             pltpu.VMEM(right_blocks.shape, BF16),
             pltpu.VMEM((STEPS, sectors, half_rows, width), BF16),
             pltpu.VMEM((STEPS, sectors, half_rows, width), BF16),
-            pltpu.VMEM((pairs * width, width), BF16),
+            pltpu.VMEM(left_blocks.shape, BF16),
             pltpu.VMEM((2, half_rows, width), F32),
             pltpu.VMEM((rows, width), F32),
             pltpu.VMEM((STEPS, chips, rows, width), BF16),
@@ -314,7 +312,7 @@
             pltpu.VMEM((STEPS + 1, ops, 2, 8, 128), F32),
             pltpu.VMEM((STEPS + 1, sectors, 2, 8, 128), F32),
             pltpu.VMEM((STEPS + 1, 2, 8, 128), F32),
-            dma((5 + pairs,)),
+            dma((6,)),
             dma((STEPS, sectors * ops)),
             dma((STEPS, sectors, chips, 2)),
             dma((STEPS, chips)),

time: 86 us -> 85.4 us (level)
  no operation moved by 1% of the time
where the time goes in v4:
time: 85.4 us; the launch traced here: 85.2 us
  Pallas kernels  81.8 us (96%)
  local copies, waits for them, and re-layouts  2.74 us (3%)
    pallas_call x1, Pallas kernels, shards(): pl.pallas_call(functools.partial(kernel, sectors, ops, entry_total), out_...  81.8 us
    unnamed x2, local copies, waits for them, and re-layouts  2.74 us

profile of v4, /device:TPU:0, one launch (start us, length us, event | category | flops | bytes accessed | tf_op | source)
XLA Modules:
  0.0 85.2 jit_solution(3916352935365828327)
XLA Ops:
  0.6 81.8 %shard_map.77 = (f32[64,512]{1,0:T(8,128)}, f32[2]{0:T(128)}) custom-call(s32[4,64]{1,0:T(4,128)} %coup_in.1, s32[4]{0:T(128)} %sizes_in.1, f32[64,512]{1,0:T(8,128)} %bitcast.3, f32[64,512]{1,0:T(8,128)} %bitcast.4, bf16[8,512,512]{2,1,0:T(8,128)(2,1)} %left.1, bf16[8,512,512]{2,1,0:T(8,128)(2,1)} %right.1), custom_call_target="tpu_custom_call" | custom-call | tf_op jit(solution)/shard_map/pallas_call | solution.py:288
  82.5 1.6 %copy.10 = f32[1,64,512]{2,1,0:T(8,128)} copy(f32[1,64,512]{2,1,0:T(8,128)} %bitcast.5) | data formatting | bytes 262144
  84.0 1.2 %copy.11 = f32[2]{0:T(128)} copy(f32[2]{0:T(128)} %get-tuple-element.9) | data formatting | bytes 16

commit v5 on v4

--- a/solution.py
+++ b/solution.py
@@ -78,8 +78,6 @@
     for d in range(1, sectors):
         pl.semaphore_signal(barrier, inc=1, device_id=(z_at[d], o), device_id_type=MESH)
 
-    for load in loads:
-        load.start()
     small[0].wait()
     small[1].wait()
     bound = sizes[z]
@@ -151,24 +149,25 @@
         def spread(d, g):
             if d or g:
                 arrive(d, g, 0)
-            order = list(range(bits)) if d % 2 == 0 else list(range(bits))[::-1]
+            order = list(range(bits)) if d < sectors // 2 else list(range(bits))[::-1]
             last = -1
             for at, bit in enumerate(order):
                 if g & (1 << bit):
                     last = at
-            if d == 0 and g == 0 and sectors > 1:
-                send(0, 0, (z_at[1], o), 1, 0, 0)
+            if d == 0 and g == 0:
+                for far in range(1, sectors):
+                    send(0, 0, (z_at[far], o), far, 0, 0)
             for bit in order[last + 1 :]:
                 send(d, g, (z, op_at[2 << bit]), d, g ^ (1 << bit), 0)
-            if d == 0 and g == 0:
-                for far in range(2, sectors):
-                    send(0, 0, (z_at[far], o), far, 0, 0)
             send(d, g, (z, op_at[1]), d, g, 1)
+            if step == 0 and d == 0 and g == 0:
+                for load in loads:
+                    load.start()
 
         level = lambda g: bin(g).count("1")
         is_late = lambda dg: dg[1] >= half and level(dg[1]) > 1
         plan = [(d, g) for d in range(sectors) for g in range(chips)]
-        plan.sort(key=lambda dg: (is_late(dg), dg[0] + level(dg[1]), dg))
+        plan.sort(key=lambda dg: (is_late(dg), dg[0] + level(dg[1]), level(dg[1]), dg))
         early = [dg for dg in plan if not is_late(dg)]
         late = [dg for dg in plan if is_late(dg)]
 
@@ -232,15 +231,14 @@
 
         acc[1] = partial(1, 0, pairs)
         to_sibling(1)
-        acc[0] = partial(0, 0, pairs // 2)
-        to_chips(1)
-        acc[0] += partial(0, pairs // 2, pairs)
+        acc[0] = partial(0, 0, pairs)
         to_sibling(0)
         sc_t[step, 0] = (
             folded(xa[step, 0].astype(F32) * acc[0]) + folded(xb[step, 0].astype(F32) * acc[1])
         )
         sc_t[step, 1] = folded(cur[...] * cur[...])
         finish = reduce_tile(step)
+        to_chips(1)
         to_chips(0)
         both = finish()
         r1(0).wait_recv()

time: 85.4 us -> 75.5 us (0.88)
  Pallas kernels: 81.8 us -> 72 us
    pallas_call x1, Pallas kernels: 81.8 us -> 72 us  [shards(): pl.pallas_call(functools.partial(kernel, sectors, ops, entry_total), out_...]
where the time goes in v5:
time: 75.5 us; the launch traced here: 75.4 us
  Pallas kernels  72 us (95%)
  local copies, waits for them, and re-layouts  2.74 us (4%)
    pallas_call x1, Pallas kernels, shards(): pl.pallas_call(functools.partial(kernel, sectors, ops, entry_total), out_...  72 us
    unnamed x2, local copies, waits for them, and re-layouts  2.74 us

profile of v5, /device:TPU:0, one launch (start us, length us, event | category | flops | bytes accessed | tf_op | source)
XLA Modules:
  0.0 75.4 jit_solution(15828641039213722948)
XLA Ops:
  0.6 72.0 %shard_map.77 = (f32[64,512]{1,0:T(8,128)}, f32[2]{0:T(128)}) custom-call(s32[4,64]{1,0:T(4,128)} %coup_in.1, s32[4]{0:T(128)} %sizes_in.1, f32[64,512]{1,0:T(8,128)} %bitcast.3, f32[64,512]{1,0:T(8,128)} %bitcast.4, bf16[8,512,512]{2,1,0:T(8,128)(2,1)} %left.1, bf16[8,512,512]{2,1,0:T(8,128)(2,1)} %right.1), custom_call_target="tpu_custom_call" | custom-call | tf_op jit(solution)/shard_map/pallas_call | solution.py:286
  72.6 1.6 %copy.10 = f32[1,64,512]{2,1,0:T(8,128)} copy(f32[1,64,512]{2,1,0:T(8,128)} %bitcast.5) | data formatting | bytes 262144
  74.2 1.2 %copy.11 = f32[2]{0:T(128)} copy(f32[2]{0:T(128)} %get-tuple-element.9) | data formatting | bytes 16

commit v6 on v2

--- a/solution.py
+++ b/solution.py
@@ -52,26 +52,33 @@
     o = lax.axis_index("op")
     m, c = o // 2, o % 2
     top = m // half
+    chip_at = [flip(m, g) for g in range(chips)]
+    op_at = [flip(o, k) for k in range(ops)]
+    z_at = [flip(z, d) for d in range(sectors)]
+    row_at = [
+        [pl.multiple_of((chip_at[g] % half) * (2 * rows) + core * rows, rows) for core in (c, 1 - c)]
+        for g in range(chips)
+    ]
+    first_at = [pl.multiple_of(at * half_rows, half_rows) for at in (top, 1 - top)]
+    valid = {r: jnp.logical_and(z + r >= 0, z + r < sectors) for r in range(1 - sectors, sectors)}
 
     small = [(wf_in, wf), (sizes_in, sizes), (coup_in, coup), (diag_in, diag)]
     small = [
         pltpu.make_async_copy(src, dst, load_sem.at[at]) for at, (src, dst) in enumerate(small)
     ]
-    loads = [pltpu.make_async_copy(right, rv, load_sem.at[4])] + [
-        pltpu.make_async_copy(left.at[p], lv.at[:, pl.ds(p * width, width)], load_sem.at[5 + p])
-        for p in range(pairs)
+    loads = [
+        pltpu.make_async_copy(right, rv, load_sem.at[4]),
+        pltpu.make_async_copy(left, lv, load_sem.at[5]),
     ]
     for load in small:
         load.start()
 
     barrier = pltpu.get_barrier_semaphore()
     for k in range(1, ops):
-        pl.semaphore_signal(barrier, inc=1, device_id=(z, flip(o, k)), device_id_type=MESH)
+        pl.semaphore_signal(barrier, inc=1, device_id=(z, op_at[k]), device_id_type=MESH)
     for d in range(1, sectors):
-        pl.semaphore_signal(barrier, inc=1, device_id=(flip(z, d), o), device_id_type=MESH)
-
-    for load in loads:
-        load.start()
+        pl.semaphore_signal(barrier, inc=1, device_id=(z_at[d], o), device_id_type=MESH)
+
     small[0].wait()
     small[1].wait()
     bound = sizes[z]
@@ -86,7 +93,7 @@
         for k in range(1, ops):
             copy = pltpu.make_async_remote_copy(
                 sc_t.at[red], sc_a.at[red, o], a_send.at[red, k], a_recv.at[red, k],
-                device_id=(z, flip(o, k)), device_id_type=MESH)
+                device_id=(z, op_at[k]), device_id_type=MESH)
             copy.start()
             sent.append(copy)
         sc_a[red, o] = sc_t[red]
@@ -94,19 +101,19 @@
         def finish():
             for k in range(1, ops):
                 pltpu.make_async_remote_copy(
-                    sc_t.at[red], sc_a.at[red, flip(o, k)], a_send.at[red, k], a_recv.at[red, k],
-                    device_id=(z, flip(o, k)), device_id_type=MESH).wait_recv()
+                    sc_t.at[red], sc_a.at[red, op_at[k]], a_send.at[red, k], a_recv.at[red, k],
+                    device_id=(z, op_at[k]), device_id_type=MESH).wait_recv()
             sc_b[red, z] = jnp.sum(sc_a[red], axis=0)
             for d in range(1, sectors):
                 copy = pltpu.make_async_remote_copy(
                     sc_b.at[red, z], sc_b.at[red, z], b_send.at[red, d], b_recv.at[red, d],
-                    device_id=(flip(z, d), o), device_id_type=MESH)
+                    device_id=(z_at[d], o), device_id_type=MESH)
                 copy.start()
                 sent.append(copy)
             for d in range(1, sectors):
                 pltpu.make_async_remote_copy(
-                    sc_b.at[red, z], sc_b.at[red, flip(z, d)], b_send.at[red, d], b_recv.at[red, d],
-                    device_id=(flip(z, d), o), device_id_type=MESH).wait_recv()
+                    sc_b.at[red, z], sc_b.at[red, z_at[d]], b_send.at[red, d], b_recv.at[red, d],
+                    device_id=(z_at[d], o), device_id_type=MESH).wait_recv()
             both = jnp.sum(sc_b[red], axis=0)
             for copy in sent:
                 copy.wait_send()
@@ -119,25 +126,23 @@
         groups = (xa.at[step], xb.at[step])
 
         def place(r, g, core):
-            chip = flip(m, g)
-            row = pl.multiple_of((chip % half) * (2 * rows) + core * rows, rows)
-            return z + r, row, 2 * chip + core
+            return z + r, row_at[g][core], op_at[2 * g + core]
 
         sent = []
 
         def inside(r):
-            return jnp.logical_and(z + r >= 0, z + r < sectors)
-
-        def send(pred, r, g, to_z, to_m, to_core, to_g):
+            return valid[r]
+
+        def send(pred, r, g, to, to_g):
             at = len(sent)
 
             def copy():
-                sector, row, owner = place(r, g, c)
+                sector, row, owner = place(r, g, 0)
                 source = groups[1 if g >= half else 0].at[sector, pl.ds(row, rows), :]
                 target = groups[1 if to_g >= half else 0].at[sector, pl.ds(row, rows), :]
                 return pltpu.make_async_remote_copy(
                     source, target, x_send.at[at], x_recv.at[step, sector, owner],
-                    device_id=(to_z, 2 * to_m + to_core), device_id_type=MESH)
+                    device_id=to, device_id_type=MESH)
 
             sent.append((pred, copy))
             pl.when(pred)(lambda: copy().start())
@@ -147,27 +152,30 @@
             slot = groups[1 if g >= half else 0].at[sector, pl.ds(row, rows), :]
             pltpu.make_async_remote_copy(
                 slot, slot, x_send.at[0], x_recv.at[step, sector, owner],
-                device_id=(z, flip(o, 1)), device_id_type=MESH).wait_recv()
-
-        own_sector, own_row, _ = place(0, 0, c)
+                device_id=(z, op_at[1]), device_id_type=MESH).wait_recv()
+
+        own_sector, own_row, _ = place(0, 0, 0)
         groups[0][own_sector, pl.ds(own_row, rows), :] = cur[...].astype(BF16)
 
         def spread(r, g):
             here = inside(r)
             if r or g:
-                pl.when(here)(lambda: arrive(r, g, c))
+                pl.when(here)(lambda: arrive(r, g, 0))
             if g == 0 and r <= 0:
-                send(jnp.logical_and(here, z + 1 < sectors), r, 0, z + 1, m, c, 0)
+                send(jnp.logical_and(here, z + 1 < sectors), r, 0, (z + 1, o), 0)
             if g == 0 and r >= 0:
-                send(jnp.logical_and(here, z >= 1), r, 0, z - 1, m, c, 0)
+                send(jnp.logical_and(here, z >= 1), r, 0, (z - 1, o), 0)
             order = list(range(bits)) if r % 2 == 0 else list(range(bits))[::-1]
             last = -1
             for at, bit in enumerate(order):
                 if g & (1 << bit):
                     last = at
             for bit in order[last + 1 :]:
-                send(here, r, g, z, flip(m, 1 << bit), c, g ^ (1 << bit))
-            send(here, r, g, z, m, 1 - c, g)
+                send(here, r, g, (z, op_at[2 << bit]), g ^ (1 << bit))
+            send(here, r, g, (z, op_at[1]), g)
+            if step == 0 and r == 0 and g == 0:
+                for load in loads:
+                    load.start()
 
         def arrive_sibling(first, end):
             for r in range(1 - sectors, sectors):
@@ -175,7 +183,7 @@
                 @pl.when(inside(r))
                 def _():
                     for g in range(first, end):
-                        arrive(r, g, 1 - c)
+                        arrive(r, g, 1)
 
         level = lambda g: bin(g).count("1")
         is_late = lambda rg: rg[1] >= half and level(rg[1]) > 1
@@ -189,7 +197,7 @@
             for p in range(pairs):
                 x = group[coup[z, o * pairs + p]]
                 t = lax.dot_general(x, rv[p], (((1,), (1,)), ((), ())), preferred_element_type=F32)
-                tt[pl.ds(pl.multiple_of(p * width + first, half_rows), half_rows), :] = t.astype(BF16)
+                tt[p, pl.ds(first, half_rows), :] = t.astype(BF16)
 
         for r, g in early:
             spread(r, g)
@@ -209,47 +217,47 @@
         def r1(g):
             return pltpu.make_async_remote_copy(
                 s1_tx.at[step, g], s1_rx.at[step, g], r1_send.at[step, g], r1_recv.at[step, g],
-                device_id=(z, 2 * m + 1 - c), device_id_type=MESH)
+                device_id=(z, op_at[1]), device_id_type=MESH)
 
         def r2(g):
             return pltpu.make_async_remote_copy(
                 s2_tx.at[step, g], s2_rx.at[step, g], r2_send.at[step, g], r2_recv.at[step, g],
-                device_id=(z, 2 * flip(m, g) + c), device_id_type=MESH)
+                device_id=(z, op_at[2 * g]), device_id_type=MESH)
 
         def block(which, g, core):
-            row = pl.multiple_of((flip(m, g) % half) * (2 * rows) + core * rows, rows)
-            return acc[which, pl.ds(row, rows), :]
-
-        def partial(which, column, end):
-            at = top if which == 0 else 1 - top
-            first = pl.multiple_of(at * half_rows, half_rows)
-            acc[which, :, column:end] = jnp.dot(
-                lv[pl.ds(first, half_rows), :], tt[:, column:end], preferred_element_type=F32)
+            return acc[which, pl.ds(row_at[g][core], rows), :]
+
+        def partial(which):
+            total = None
+            for p in range(pairs):
+                part = jnp.dot(
+                    lv[p, pl.ds(first_at[which], half_rows), :], tt[p], preferred_element_type=F32)
+                total = part if total is None else total + part
+            acc[which] = total
 
         def to_sibling(which):
             for g in reversed(range(which * half, which * half + half)):
-                s1_tx[step, g] = block(which, g, 1 - c).astype(BF16)
+                s1_tx[step, g] = block(which, g, 1).astype(BF16)
                 r1(g).start()
 
         def to_chips(which):
             for g in reversed(range(max(1, which * half), which * half + half)):
                 r1(g).wait_recv()
-                s2_tx[step, g] = (block(which, g, c) + s1_rx[step, g].astype(F32)).astype(BF16)
+                s2_tx[step, g] = (block(which, g, 0) + s1_rx[step, g].astype(F32)).astype(BF16)
                 r2(g).start()
 
-        partial(1, 0, width)
+        partial(1)
         to_sibling(1)
-        partial(0, 0, width // 2)
-        to_chips(1)
-        partial(0, width // 2, width)
+        partial(0)
         to_sibling(0)
         sc_t[step, 0] = folded(xa[step, z].astype(F32) * acc[0]) + folded(xb[step, z].astype(F32) * acc[1])
         sc_t[step, 1] = folded(cur[...] * cur[...])
         finish = reduce_tile(step)
+        to_chips(1)
         to_chips(0)
         both = finish()
         r1(0).wait_recv()
-        sigma = block(0, 0, c) + s1_rx[step, 0].astype(F32)
+        sigma = block(0, 0, 0) + s1_rx[step, 0].astype(F32)
         for g in range(1, chips):
             r2(g).wait_recv()
             sigma = sigma + s2_rx[step, g].astype(F32)
@@ -304,11 +312,11 @@
             pltpu.SMEM(sector_sizes.shape, jnp.int32),
             pltpu.VMEM((rows, width), F32),
             pltpu.VMEM((rows, width), F32),
-            pltpu.VMEM((width, pairs * width), BF16),
+            pltpu.VMEM(left_blocks.shape, BF16),
             pltpu.VMEM(right_blocks.shape, BF16),
             pltpu.VMEM((STEPS, sectors, half_rows, width), BF16),
             pltpu.VMEM((STEPS, sectors, half_rows, width), BF16),
-            pltpu.VMEM((pairs * width, width), BF16),
+            pltpu.VMEM(left_blocks.shape, BF16),
             pltpu.VMEM((2, half_rows, width), F32),
             pltpu.VMEM((rows, width), F32),
             pltpu.VMEM((STEPS, chips, rows, width), BF16),
@@ -318,7 +326,7 @@
             pltpu.VMEM((STEPS + 1, ops, 2, 8, 128), F32),
             pltpu.VMEM((STEPS + 1, sectors, 2, 8, 128), F32),
             pltpu.VMEM((STEPS + 1, 2, 8, 128), F32),
-            dma((5 + pairs,)),
+            dma((6,)),
             dma((sends,)),
             dma((STEPS, sectors, ops)),
             dma((STEPS, chips)),

time: 81.1 us -> 78.2 us (0.964)
  Pallas kernels: 77.5 us -> 74.7 us
    pallas_call x1, Pallas kernels: 77.5 us -> 74.7 us  [shards(): pl.pallas_call(functools.partial(kernel, sectors, ops, entry_total), out_...]
where the time goes in v6:
time: 78.2 us; the launch traced here: 78 us
  Pallas kernels  74.7 us (96%)
  local copies, waits for them, and re-layouts  2.74 us (4%)
    pallas_call x1, Pallas kernels, shards(): pl.pallas_call(functools.partial(kernel, sectors, ops, entry_total), out_...  74.7 us
    unnamed x2, local copies, waits for them, and re-layouts  2.74 us

profile of v6, /device:TPU:0, one launch (start us, length us, event | category | flops | bytes accessed | tf_op | source)
XLA Modules:
  0.0 78.0 jit_solution(15257943448054833763)
XLA Ops:
  0.6 74.7 %shard_map.77 = (f32[64,512]{1,0:T(8,128)}, f32[2]{0:T(128)}) custom-call(s32[4,64]{1,0:T(4,128)} %coup_in.1, s32[4]{0:T(128)} %sizes_in.1, f32[64,512]{1,0:T(8,128)} %bitcast.3, f32[64,512]{1,0:T(8,128)} %bitcast.4, bf16[8,512,512]{2,1,0:T(8,128)(2,1)} %left.1, bf16[8,512,512]{2,1,0:T(8,128)(2,1)} %right.1), custom_call_target="tpu_custom_call" | custom-call | tf_op jit(solution)/shard_map/pallas_call | solution.py:302
  75.3 1.6 %copy.10 = f32[1,64,512]{2,1,0:T(8,128)} copy(f32[1,64,512]{2,1,0:T(8,128)} %bitcast.5) | data formatting | bytes 262144
  76.9 1.2 %copy.11 = f32[2]{0:T(128)} copy(f32[2]{0:T(128)} %get-tuple-element.9) | data formatting | bytes 16
